TPU v7x, 128 devices: a whole 4x4x4 slice. The times are simulated.
128 devices in a mesh: pipe: 16 (over x_lo, z, core), tensor: 8 (over x_hi, y).
Axes of the slice: x: 4 (x_hi: 2, x_lo: 2; x = x_hi * 2 + x_lo), y: 4, z: 4, core: 2. Of those that a mesh axis runs over, the one named last changes fastest.
Arguments:
- stashed: bfloat16 [16, 2, 512, 4096], P('pipe', None, 'tensor'), may hold values from -64 to 64
- upstream: bfloat16 [16, 512, 4096], P('pipe', 'tensor'), may hold values from -6 to 6
- loss_grad: bfloat16 [512, 4096], P('tensor'), may hold values from -6 to 6
- norm_gain: float32 [16, 4096], P('pipe'), may hold values from 0.5 to 1.5
- w_query: bfloat16 [16, 4096, 4096], P('pipe', None, 'tensor'), may hold values from -0.09375 to 0.09375
- w_key: bfloat16 [16, 4096, 1024], P('pipe', None, 'tensor'), may hold values from -2.359375 to 2.359375
- w_value: bfloat16 [16, 4096, 1024], P('pipe', None, 'tensor'), may hold values from -0.09375 to 0.09375
- w_out: bfloat16 [16, 4096, 4096], P('pipe', 'tensor'), may hold values from -0.09375 to 0.09375
- evicted_map: int32 [16], replicated, may hold values from 0 to 1, as said below
- plan: int32 [17], replicated, may hold values from 0 to 16, each once
- segments: int32 [17, 512], replicated, may hold values from 0 to 3, never falling along the last dimension, each value on 1 to 256 neighbouring positions
Outputs:
- layer_grads: bfloat16 [16, 2, 512, 4096], P('pipe', None, 'tensor')
Inputs may be any that keep to these rules, and one draw needn't show every extreme that they name: `evicted_map`: entry i equals entry 15 - i and entry 0 is 1; where entry i is 1, stashed[i] holds the inputs of section 15 - i.
All inputs are finite; a program needn't handle non-finite values.
Results may differ from a plain program's by a relative error of at most 0.023.
The roundings to bfloat16 on the way count: a program that leaves them out, or rounds other values in their place, can miss the bound.
Values may be sent and summed in bfloat16 or wider, within the bound.
A program may use at most 128 MiB of HBM per device.

v0:
```python
import math

import jax
import jax.numpy as jnp
from jax import lax
from jax.experimental import pallas as pl
from jax.experimental.pallas import tpu as pltpu
from jax.sharding import PartitionSpec as P

MESH = pl.DeviceIdType.MESH
HD = 128
EPS = 1e-05
F32 = jnp.float32
BF16 = jnp.bfloat16


ORDER = (
    61, 0, 28, 12, 13, 2, 4, 27, 62, 65, 60, 1,
    19, 20, 11, 3, 18, 52, 53, 54, 66, 24, 23, 26,
    22, 58, 31, 57, 7, 55, 56, 30, 64, 5, 32, 10,
    29, 59, 8, 21, 25, 126, 6, 63, 33, 87, 68, 88,
    67, 34, 36, 125, 70, 35, 37, 130, 124, 91, 69, 92,
    71, 129, 38, 39, 40, 41, 72, 75, 74, 9, 73, 42,
    44, 43, 45, 46, 76, 78, 79, 131, 77, 80, 49, 50,
    47, 48, 81, 83, 82, 84, 51, 14, 86, 127, 128, 85,
    16, 15, 96, 95, 89, 93, 17, 134, 94, 101, 90, 132,
    133, 102, 99, 140, 138, 139, 103, 142, 100, 97, 141, 98,
    135, 104, 106, 137, 136, 144, 105, 107, 143, 145, 146, 147,
    148, 149, 108, 111, 150, 113, 110, 109, 152, 153, 154, 155,
    151, 114, 116, 112, 156, 115, 117, 157, 158, 159, 160, 118,
    121, 119, 120, 122, 161, 123,
)
ALONG = ()
MIXED = ("E", "T", )


class Steps:
    def __init__(self, send, recv):
        self.send, self.recv = send, recv
        self.copies, self.needs, self.work = {}, {}, {}
        self.arrived, self.left, self.ran = set(), set(), set()

    def copy(self, name, needs, src, dst, device):
        i = len(self.copies)
        self.needs[name] = tuple(needs)
        self.copies[name] = pltpu.make_async_remote_copy(
            src_ref=src,
            dst_ref=dst,
            send_sem=self.send.at[i],
            recv_sem=self.recv.at[i],
            device_id=device,
            device_id_type=MESH,
        )

    def step(self, name, needs, work):
        self.needs[name] = tuple(needs)
        self.work[name] = work

    def arrive(self, name):
        if name not in self.arrived:
            self.arrived.add(name)
            self.copies[name].wait_recv()

    def leave(self, name):
        if name not in self.left:
            self.left.add(name)
            self.copies[name].wait_send()

    def run(self, order):
        names = list(self.needs)
        assert sorted(order) == list(range(len(names)))
        for i in order:
            name = names[i]
            for need in self.needs[name]:
                assert need in self.ran
                if need in self.copies:
                    self.arrive(need)
            if name in self.copies:
                self.copies[name].start()
            else:
                self.work[name]()
            self.ran.add(name)
        for name in self.copies:
            self.arrive(name)
            self.leave(name)


def kernel(
    stash, upstream, loss, gain, wq, wk, wv, wo, evicted, plan, segs, out,
    w, wout, h0, d0, h1, d1, part, r0, r1, own, mir, lossv, pas, res,
    qs, ogs, kk, vv, dqkv, dk_acc, dv_acc, bias, probs, wt, lsem, ssem, rsem,
):
    p, t = lax.axis_index("pipe"), lax.axis_index("tensor")
    xh, y = t // 4, t % 4
    yp, ym, y2 = (y + 1) % 4, (y + 3) % 4, (y + 2) % 4
    xo = 1 - xh
    to_yp, to_ym, to_x = (p, xh * 4 + yp), (p, xh * 4 + ym), (p, xo * 4 + y)
    to_mirror, to_prev, from_next = (15 - p, t), ((p + 15) % 16, t), ((p + 1) % 16, t)
    steps = Steps(ssem, rsem)

    def rows(a, b, h):
        return pl.ds(pl.multiple_of(h * 256 + (a * 4 + b) * 32, 32), 32)

    def part_rows(a, b, h, q):
        return pl.ds(pl.multiple_of(h * 256 + (a * 4 + b) * 32 + 16 * q, 16), 16)

    def half(h):
        return pl.ds(256 * h, 256)

    barrier = pltpu.get_barrier_semaphore()
    for device in (to_yp, to_ym, to_x, to_mirror, from_next):
        pl.semaphore_signal(barrier, inc=1, device_id=device, device_id_type=MESH)

    local = [
        pltpu.make_async_copy(upstream.at[0, 0:32], d0.at[rows(xh, y, 0)], lsem.at[0]),
        pltpu.make_async_copy(upstream.at[0, 32:64], d0.at[rows(xh, y, 1)], lsem.at[1]),
        pltpu.make_async_copy(stash.at[0], own, lsem.at[2]),
        pltpu.make_async_copy(wo.at[0], wout, lsem.at[3]),
        pltpu.make_async_copy(wq.at[0], w.at[:, 0:512], lsem.at[4]),
        pltpu.make_async_copy(wk.at[0], w.at[:, 512:640], lsem.at[5]),
        pltpu.make_async_copy(wv.at[0], w.at[:, 640:768], lsem.at[6]),
        pltpu.make_async_copy(loss, lossv, lsem.at[7]),
    ]
    for c in local:
        c.start()
    pl.semaphore_wait(barrier, 5)

    def gather(name, g, h, needs, along=False):
        def cp(part, after, sl, device, cols=None):
            at = g.at[sl] if cols is None else g.at[sl, pl.ds(2048 * cols, 2048)]
            steps.copy(name + part, after, at, at, device)

        cp("x", needs, rows(xh, y, h), to_x)
        cp("ap", needs, rows(xh, y, h), to_yp)
        cp("am", needs, rows(xh, y, h), to_ym)
        if name[0] in MIXED and h == 0:
            cp("bp", [name + "x"], part_rows(xo, y, h, 0), to_yp)
            cp("bp2", [name + "x"], part_rows(xo, y, h, 1), to_yp, 0)
            cp("f", [name + "ap"], part_rows(xh, ym, h, 1), to_x, 1)
        else:
            cp("bp", [name + "x"], rows(xo, y, h), to_yp)
        if name[0] in MIXED and h == 1:
            cp("bm", [name + "x"], part_rows(xo, y, h, 1), to_ym)
            cp("bm2", [name + "x"], part_rows(xo, y, h, 0), to_ym, 0)
            cp("f", [name + "am"], part_rows(xh, yp, h, 0), to_x, 1)
        else:
            cp("bm", [name + "x"], rows(xo, y, h), to_ym)
        cp("cp", [name + "ap"], part_rows(xh, ym, h, 0), to_yp)
        cp("cm", [name + "am"], part_rows(xh, yp, h, 1), to_ym)
        if along:
            cp("ep", [name + "bp"], part_rows(xo, ym, h, 0), to_yp)
            cp("em", [name + "bm"], part_rows(xo, yp, h, 1), to_ym)
        else:
            cp("e", [name + "cp", name + "cm"], rows(xh, y2, h), to_x)
        return [n for n in steps.copies if n.startswith(name)]

    def scatter(name, r, h, needs):
        def cp(part_name, after, sl, lo, n, device):
            steps.copy(name + part_name, after, part.at[sl], r.at[pl.ds(224 * h + lo, n)], device)

        def add(step, after, *sums):
            def work():
                for sl, n, first, end, los in sums:

                    def body(i, carry):
                        cols = pl.ds(pl.multiple_of(i * 512, 512), 512)
                        total = part[sl, cols].astype(F32)
                        for lo in los:
                            total = total + r[pl.ds(224 * h + lo, n), cols].astype(F32)
                        part[sl, cols] = total.astype(BF16)
                        return carry

                    lax.fori_loop(first, end, body, 0)

            steps.step(name + step, after, work)

        mixed = name[0] in MIXED

        def first(n, sl, lo, device, rows_of=32, cols=(0, 4096)):
            at = pl.ds(*cols)
            steps.copy(name + n, needs, part.at[sl, at], r.at[pl.ds(224 * h + lo, rows_of), at], device)

        first("e", rows(xo, y2, h), 0, to_x)
        if mixed and h == 0:
            first("bm", part_rows(xo, ym, h, 0), 32, to_ym, 16)
            first("bm2", part_rows(xo, ym, h, 1), 48, to_ym, 16, (0, 2048))
            first("f", part_rows(xo, ym, h, 1), 48, to_x, 16, (2048, 2048))
        else:
            first("bm", rows(xo, ym, h), 32, to_ym)
        if mixed and h == 1:
            first("bp", part_rows(xo, yp, h, 1), 80, to_yp, 16)
            first("bp2", part_rows(xo, yp, h, 0), 64, to_yp, 16, (0, 2048))
            first("f", part_rows(xo, yp, h, 0), 64, to_x, 16, (2048, 2048))
        else:
            first("bp", rows(xo, yp, h), 64, to_yp)
        add("far", [name + "e"], (rows(xh, y2, h), 32, 0, 8, (0,)))
        cp("cm", [name + "far"], part_rows(xh, y2, h, 0), 96, 16, to_ym)
        cp("cp", [name + "far"], part_rows(xh, y2, h, 1), 112, 16, to_yp)
        twos = [name + n for n in ("bm", "bp")]
        if not mixed:
            add("acr", twos, (rows(xo, y, h), 32, 0, 8, (32, 64)))
        elif h == 0:
            add(
                "acr", [*twos, name + "bm2"],
                (part_rows(xo, y, h, 0), 16, 0, 8, (32, 64)),
                (part_rows(xo, y, h, 1), 16, 0, 4, (48, 80)),
                (part_rows(xo, y, h, 1), 16, 4, 8, (80,)),
            )
        else:
            add(
                "acr", [*twos, name + "bp2"],
                (part_rows(xo, y, h, 1), 16, 0, 8, (48, 80)),
                (part_rows(xo, y, h, 0), 16, 0, 4, (32, 64)),
                (part_rows(xo, y, h, 0), 16, 4, 8, (32,)),
            )
        cp("x", [name + "acr"], rows(xo, y, h), 192, 32, to_x)
        via_m, via_p = [], []
        if mixed and h == 0:
            via_m = [(part_rows(xh, ym, h, 1), 16, 4, 8, (48,))]
        if mixed and h == 1:
            via_p = [(part_rows(xh, yp, h, 0), 16, 4, 8, (64,))]
        add("nrm", [name + "cm", *needs] + [name + "f"] * len(via_m), (part_rows(xh, ym, h, 0), 16, 0, 8, (96,)), *via_m)
        cp("am", [name + "nrm"], rows(xh, ym, h), 128, 32, to_ym)
        add("nrp", [name + "cp", *needs] + [name + "f"] * len(via_p), (part_rows(xh, yp, h, 1), 16, 0, 8, (112,)), *via_p)
        cp("ap", [name + "nrp"], rows(xh, yp, h), 160, 32, to_yp)
        return [name + n for n in ("am", "ap", "x", "far", "acr", "nrm", "nrp")]

    flipped = evicted[p] == 1
    gain_row = gain[...]
    nt = (((1,), (1,)), ((), ()))
    scale = 1.0 / math.sqrt(HD)

    def norm(m, h, g):
        def body(n, carry):
            lo = 32 * h + n * 16
            sl = pl.ds(pl.multiple_of(lo, 16), 16)
            x = jnp.where(flipped, mir[m, sl].astype(F32), own[m, sl].astype(F32))
            own[m, sl] = x.astype(BF16)
            inverse = 1.0 / jnp.sqrt(jnp.mean(x * x, axis=-1, keepdims=True) + EPS)
            g[pl.ds(pl.multiple_of(256 * h + t * 32 + n * 16, 16), 16)] = (x * inverse * gain_row).astype(BF16)
            return carry

        lax.fori_loop(0, 2, body, 0)

    def norm_back(m, h, g, r):
        def body(n, carry):
            lo = n * 16
            sl = pl.ds(pl.multiple_of(h * 32 + lo, 16), 16)
            row = pl.ds(pl.multiple_of(256 * h + t * 32 + lo, 16), 16)
            total = part[row].astype(F32)
            for i in (128, 160, 192):
                total = total + r[pl.ds(pl.multiple_of(224 * h + i + lo, 16), 16)].astype(F32)
            x = own[m, sl].astype(F32)
            inverse = 1.0 / jnp.sqrt(jnp.mean(x * x, axis=-1, keepdims=True) + EPS)
            normed = x * inverse
            scaled = total * gain_row
            result = inverse * (scaled - normed * jnp.mean(scaled * normed, axis=-1, keepdims=True))
            res[m, sl] = (result + g[row].astype(F32)).astype(BF16)
            return carry

        lax.fori_loop(0, 2, body, 0)

    def project(g, h):
        r = jnp.dot(g[half(h)], w[...], preferred_element_type=F32).astype(BF16)
        for j in range(4):
            qs[pl.ds(j * 512 + 256 * h, 256)] = r[:, j * HD : (j + 1) * HD]
        kk[half(h)] = r[:, 512:640]
        vv[half(h)] = r[:, 640:768]

    def back_out(g, h):
        r = lax.dot_general(g[half(h)], wout[...], nt, preferred_element_type=F32).astype(BF16)
        for j in range(4):
            ogs[pl.ds(j * 512 + 256 * h, 256)] = r[:, j * HD : (j + 1) * HD]

    def position(r):
        return ((r & 255) >> 5) * 64 + (r >> 8) * 32 + (r & 31)

    def mask(m):
        plain = jnp.broadcast_to(segs[pl.ds(plan[p + m], 1)], (8, 512))
        seg_row = jnp.concatenate([plain[:, 64 * i + 32 * h : 64 * i + 32 * h + 32] for h in (0, 1) for i in range(8)], axis=1)
        seg_col = jnp.broadcast_to(seg_row[:1], (128, 512)).T[:, :1]
        kpos = position(lax.broadcasted_iota(jnp.int32, (512, 256), 0))
        for h in (0, 1):
            qpos = position(lax.broadcasted_iota(jnp.int32, (512, 256), 1) + 256 * h)
            allowed = (kpos <= qpos) & (seg_col == seg_row[:1, 256 * h : 256 * h + 256])
            bias[m, h] = jnp.where(allowed, 0.0, -1e30)

    def forward(m, h):
        def head(j, carry):
            q = qs[pl.ds(pl.multiple_of(j * 512 + h * 256, 256), 256)]
            scores = lax.dot_general(kk[...], q, nt, preferred_element_type=F32) * scale
            scores = scores + bias[m, h]
            weights = jnp.exp(scores - jnp.max(scores, axis=0, keepdims=True))
            probs[j, h] = weights * (1.0 / jnp.sum(weights, axis=0, keepdims=True))
            return carry

        lax.fori_loop(0, 4, head, 0)

    def backward(h):
        if h == 0:
            dk_acc[...] = jnp.zeros_like(dk_acc)
            dv_acc[...] = jnp.zeros_like(dv_acc)

        def head(j, carry):
            sl = pl.ds(pl.multiple_of(j * 512 + h * 256, 256), 256)
            q, og = qs[sl], ogs[sl]
            weights = probs[j, h]
            weight_grad = lax.dot_general(vv[...], og, nt, preferred_element_type=F32)
            delta = jnp.sum(weights * weight_grad, axis=0, keepdims=True)
            score_grad = (weights * (weight_grad - delta) * scale).astype(BF16)
            dv_acc[...] += jnp.dot(weights.astype(BF16), og, preferred_element_type=F32)
            dk_acc[...] += jnp.dot(score_grad, q, preferred_element_type=F32)
            dq = jnp.dot(kk[...].T, score_grad, preferred_element_type=F32)
            dqkv[j, half(h)] = dq.T.astype(BF16)
            return carry

        lax.fori_loop(0, 4, head, 0)
        if h == 1:
            dqkv[4] = dk_acc[...].astype(BF16)
            dqkv[5] = dv_acc[...].astype(BF16)

    def back_in(h):
        lhs = jnp.concatenate([dqkv[j, half(h)] for j in range(6)], axis=1)

        def body(n, carry):
            cols = pl.ds(pl.multiple_of(n * 512, 512), 512)
            part[half(h), cols] = jnp.dot(lhs, wt[:, cols], preferred_element_type=F32).astype(BF16)
            return carry

        lax.fori_loop(0, 8, body, 0)

    def passed(h):
        sl = pl.ds(32 * h, 32)
        d1[rows(xh, y, h)] = jnp.where(last, lossv[sl].astype(F32), pas[sl].astype(F32)).astype(BF16)

    last = p == 15
    waited = set()

    def here(*ids):
        for i in ids:
            if i not in waited:
                waited.add(i)
                local[i].wait()

    outs = [
        [pltpu.make_async_copy(res.at[m, pl.ds(32 * h, 32)], out.at[0, m, pl.ds(32 * h, 32)], lsem.at[8 + 2 * m + h]) for h in (0, 1)]
        for m in (0, 1)
    ]

    def do_norm(m, h):
        here(2)
        norm(m, h, (h0, h1)[m])

    def do_project(m, h):
        here(4, 5, 6)
        project((h0, h1)[m], h)

    def turn(i):
        here(4, 5, 6)

        def body(n, carry):
            sl = pl.ds(pl.multiple_of(1024 * i + 256 * n, 256), 256)
            wt[:, sl] = w[sl].T
            return carry

        lax.fori_loop(0, 4, body, 0)

    def do_back_out(m, h):
        here(3)
        back_out((d0, d1)[m], h)

    def do_back_in(m, h):
        if m:
            for n in [n for n in steps.copies if n.startswith("S%d" % h)]:
                steps.leave(n)
        back_in(h)

    def do_norm_back(m, h):
        norm_back(m, h, (d0, d1)[m], (r0, r1)[m])
        outs[m][h].start()

    def do_passed(h):
        here(7)
        passed(h)

    both = (0, 1)
    for m in both:
        for h in both:
            sl = pl.ds(32 * h, 32)
            steps.copy("M%d%d" % (m, h), [], stash.at[0, m, sl], mir.at[m, sl], to_mirror)
            steps.step("norm%d%d" % (m, h), ["M%d%d" % (m, h)], lambda m=m, h=h: do_norm(m, h))
        steps.step("mask%d" % m, [], lambda m=m: mask(m))
    for i in range(4):
        steps.step("wt%d" % i, [], lambda i=i: turn(i))
    for h in both:
        sl = pl.ds(32 * h, 32)
        steps.copy("P%d" % h, ["nb0%d" % h], res.at[0, sl], pas.at[sl], to_prev)
        steps.step("psd%d" % h, ["P%d" % h], lambda h=h: do_passed(h))
    for m in both:
        prev = ["bwd01"] if m else []
        for h in both:
            ins = gather("HI"[m] + str(h), (h0, h1)[m], h, ["norm%d%d" % (m, h)])
            grads = gather("DE"[m] + str(h), (d0, d1)[m], h, ["psd%d" % h] if m else [], "DE"[m] + str(h) in ALONG)
            steps.step("proj%d%d" % (m, h), ins + prev, lambda m=m, h=h: do_project(m, h))
            steps.step("bout%d%d" % (m, h), grads + prev, lambda m=m, h=h: do_back_out(m, h))
            steps.step(
                "fwd%d%d" % (m, h), ["proj%d0" % m, "proj%d1" % m, "mask%d" % m, *prev], lambda m=m, h=h: forward(m, h)
            )
            steps.step(
                "bwd%d%d" % (m, h),
                ["fwd%d%d" % (m, h), "bout%d%d" % (m, h)] + (["bwd%d0" % m] if h else []) + (["bin00", "bin01"] if m else []),
                lambda h=h: backward(h),
            )
            ready = ["bwd%d0" % m, "bwd%d1" % m, "wt0", "wt1", "wt2", "wt3"] + (["nb00", "nb01"] if m else [])
            steps.step("bin%d%d" % (m, h), ready, lambda m=m, h=h: do_back_in(m, h))
            sums = scatter("ST"[m] + str(h), (r0, r1)[m], h, ["bin%d%d" % (m, h)])
            steps.step("nb%d%d" % (m, h), sums, lambda m=m, h=h: do_norm_back(m, h))

    here(0, 1)
    steps.run(ORDER)
    here(*range(8))
    for m in both:
        for h in both:
            outs[m][h].wait()


def on_device(stashed, upstream, loss_grad, norm_gain, w_query, w_key, w_value, w_out, evicted_map, plan, segments):
    hbm = pl.BlockSpec(memory_space=pl.ANY)
    vmem = pl.BlockSpec(memory_space=pltpu.VMEM)
    smem = pl.BlockSpec(memory_space=pltpu.SMEM)
    full = pltpu.VMEM((512, 4096), BF16)
    return pl.pallas_call(
        kernel,
        name="relay_backward",
        out_shape=jax.ShapeDtypeStruct((1, 2, 64, 4096), BF16),
        in_specs=[hbm, hbm, hbm, vmem, hbm, hbm, hbm, hbm, smem, smem, vmem],
        out_specs=hbm,
        scratch_shapes=[
            pltpu.VMEM((4096, 768), BF16),
            full, full, full, full, full, full,
            pltpu.VMEM((448, 4096), BF16),
            pltpu.VMEM((448, 4096), BF16),
            pltpu.VMEM((2, 64, 4096), BF16),
            pltpu.VMEM((2, 64, 4096), BF16),
            pltpu.VMEM((64, 4096), BF16),
            pltpu.VMEM((64, 4096), BF16),
            pltpu.VMEM((2, 64, 4096), BF16),
            pltpu.VMEM((2048, HD), BF16),
            pltpu.VMEM((2048, HD), BF16),
            pltpu.VMEM((512, HD), BF16),
            pltpu.VMEM((512, HD), BF16),
            pltpu.VMEM((6, 512, HD), BF16),
            pltpu.VMEM((512, HD), F32),
            pltpu.VMEM((512, HD), F32),
            pltpu.VMEM((2, 2, 512, 256), F32),
            pltpu.VMEM((4, 2, 512, 256), F32),
            pltpu.VMEM((768, 4096), BF16),
            pltpu.SemaphoreType.DMA((12,)),
            pltpu.SemaphoreType.DMA((110,)),
            pltpu.SemaphoreType.DMA((110,)),
        ],
        compiler_params=pltpu.CompilerParams(
            collective_id=0, has_side_effects=True, vmem_limit_bytes=60 * 2**20
        ),
        cost_estimate=pl.CostEstimate(flops=20 * 10**9, bytes_accessed=16 * 2**20, transcendentals=2 * 10**6),
    )(stashed, upstream, loss_grad, norm_gain, w_query, w_key, w_value, w_out, evicted_map, plan, segments)


def solution(mesh):
    in_specs = (
        P("pipe", None, "tensor", None),
        P("pipe", "tensor", None),
        P("tensor", None),
        P("pipe", None),
        P("pipe", None, "tensor"),
        P("pipe", None, "tensor"),
        P("pipe", None, "tensor"),
        P("pipe", "tensor", None),
        P(),
        P(),
        P(),
    )
    return jax.shard_map(
        on_device, mesh=mesh, in_specs=in_specs, out_specs=P("pipe", None, "tensor", None), check_vma=False
    )
```

profile of v0, /device:TPU:0, one launch (start us, length us, event | category | flops | bytes accessed | tf_op | source)
XLA Modules:
  0.0 198.3 jit_solution(4435692845167027756)
XLA Ops:
  0.0 196.0 %relay_backward.1 = bf16[1,2,64,4096]{3,2,1,0:T(8,128)(2,1)} custom-call(bf16[1,2,64,4096]{3,2,1,0:T(8,128)(2,1)} %stash.1, bf16[1,64,4096]{2,1,0:T(8,128)(2,1)} %upstream.1, bf16[64,4096]{1,0:T(8,128)(2,1)} %loss.1, f32[1,4096]{1,0:T(1,128)} %gain.1, bf16[1,4096,512]{2,1,0:T(8,128)(2,1)} %wq.1, bf16[1,4096,128]{2,1,0:T(8,128)(2,1)} %wk.1, ...), custom_call_target="tpu_custom_call" | custom-call | flops 20000000000 | bytes 16777216 | tf_op jit(solution)/shard_map/relay_backward/pallas_call | solution.py:432
  196.0 2.3 %copy.13 = bf16[1,2,64,4096]{3,2,1,0:T(8,128)(2,1)} copy(bf16[1,2,64,4096]{3,2,1,0:T(8,128)(2,1)} %relay_backward.1) | data formatting | bytes 2097152
where the time goes:
time: 198 us
  Pallas kernels  196 us (99%)
  local copies, waits for them, and re-layouts  2.29 us (1%)
    pallas_call x1, Pallas kernels, on_device(): pl.pallas_call(kernel, name='relay_backward', out_shape=jax.ShapeDtypeStr...  196 us

commit v1 on v0

--- a/solution.py
+++ b/solution.py
@@ -15,20 +15,20 @@
 
 
 ORDER = (
-    61, 0, 28, 12, 13, 2, 4, 27, 62, 65, 60, 1,
-    19, 20, 11, 3, 18, 52, 53, 54, 66, 24, 23, 26,
-    22, 58, 31, 57, 7, 55, 56, 30, 64, 5, 32, 10,
-    29, 59, 8, 21, 25, 126, 6, 63, 33, 87, 68, 88,
-    67, 34, 36, 125, 70, 35, 37, 130, 124, 91, 69, 92,
-    71, 129, 38, 39, 40, 41, 72, 75, 74, 9, 73, 42,
-    44, 43, 45, 46, 76, 78, 79, 131, 77, 80, 49, 50,
-    47, 48, 81, 83, 82, 84, 51, 14, 86, 127, 128, 85,
-    16, 15, 96, 95, 89, 93, 17, 134, 94, 101, 90, 132,
-    133, 102, 99, 140, 138, 139, 103, 142, 100, 97, 141, 98,
-    135, 104, 106, 137, 136, 144, 105, 107, 143, 145, 146, 147,
-    148, 149, 108, 111, 150, 113, 110, 109, 152, 153, 154, 155,
-    151, 114, 116, 112, 156, 115, 117, 157, 158, 159, 160, 118,
-    121, 119, 120, 122, 161, 123,
+    27, 0, 28, 11, 62, 12, 13, 61, 2, 1, 20, 19,
+    26, 9, 3, 52, 31, 66, 54, 53, 18, 23, 60, 30,
+    7, 29, 55, 57, 24, 5, 22, 58, 10, 25, 56, 63,
+    8, 59, 4, 21, 64, 65, 32, 6, 33, 88, 34, 125,
+    126, 67, 68, 36, 35, 37, 87, 129, 70, 92, 124, 69,
+    130, 71, 38, 39, 41, 40, 91, 72, 74, 75, 73, 42,
+    44, 43, 45, 76, 77, 46, 78, 47, 49, 50, 48, 81,
+    131, 83, 82, 79, 80, 84, 51, 128, 127, 14, 93, 15,
+    86, 85, 16, 95, 96, 17, 94, 134, 133, 102, 90, 101,
+    132, 99, 89, 138, 103, 140, 139, 142, 100, 97, 104, 135,
+    98, 141, 106, 136, 144, 137, 105, 107, 143, 145, 146, 147,
+    148, 149, 150, 108, 110, 109, 113, 111, 152, 153, 154, 151,
+    114, 155, 115, 116, 156, 112, 117, 159, 160, 157, 158, 121,
+    118, 122, 119, 120, 161, 123,
 )
 ALONG = ()
 MIXED = ("E", "T", )

time: 198 us -> 202 us (1.020)
  Pallas kernels: 196 us -> 200 us
    pallas_call x1, Pallas kernels: 196 us -> 200 us  [on_device(): pl.pallas_call(kernel, name='relay_backward', out_shape=jax.ShapeDtypeStr...]
where the time goes in v1:
time: 202 us
  Pallas kernels  200 us (99%)
  local copies, waits for them, and re-layouts  2.29 us (1%)
    pallas_call x1, Pallas kernels, on_device(): pl.pallas_call(kernel, name='relay_backward', out_shape=jax.ShapeDtypeStr...  200 us

profile of v1, /device:TPU:0, one launch (start us, length us, event | category | flops | bytes accessed | tf_op | source)
XLA Modules:
  0.0 202.0 jit_solution(7603276642022773813)
XLA Ops:
  0.0 199.7 %relay_backward.1 = bf16[1,2,64,4096]{3,2,1,0:T(8,128)(2,1)} custom-call(bf16[1,2,64,4096]{3,2,1,0:T(8,128)(2,1)} %stash.1, bf16[1,64,4096]{2,1,0:T(8,128)(2,1)} %upstream.1, bf16[64,4096]{1,0:T(8,128)(2,1)} %loss.1, f32[1,4096]{1,0:T(1,128)} %gain.1, bf16[1,4096,512]{2,1,0:T(8,128)(2,1)} %wq.1, bf16[1,4096,128]{2,1,0:T(8,128)(2,1)} %wk.1, ...), custom_call_target="tpu_custom_call" | custom-call | flops 20000000000 | bytes 16777216 | tf_op jit(solution)/shard_map/relay_backward/pallas_call | solution.py:432
  199.7 2.3 %copy.13 = bf16[1,2,64,4096]{3,2,1,0:T(8,128)(2,1)} copy(bf16[1,2,64,4096]{3,2,1,0:T(8,128)(2,1)} %relay_backward.1) | data formatting | bytes 2097152
